TPU v7x, 32 devices: a whole 2x2x4 slice. The times are simulated.
32 devices in a mesh: win: 1, doc: 32 (over z, y, x, core), layer: 1.
Axes of the slice: x: 2, y: 2, z: 4, core: 2. Of those that a mesh axis runs over, the one named last changes fastest.
Arguments:
- pool_grads: bfloat16 [2, 16384, 4096], P('layer', ('win', 'doc')), may hold values from -6 to 6
- doc_ids: int32 [32, 512], P(('win', 'doc')), may hold values from 0 to 511, each once within a row
- query_grads: bfloat16 [2, 4096, 512], P('layer', 'doc'), may hold values from -6 to 6
- u_out: float32 [2, 64, 64], P('layer'), may hold values from -0.75 to 0.75
- u_in: float32 [2, 64, 64], P('layer'), may hold values from -0.75 to 0.75
- eigval: float32 [2, 64, 64], P('layer'), may hold values from 0.05 to 5
Outputs:
- scores: float32 [512, 16384], P('layer', ('win', 'doc'))
Inputs may be any that keep to these rules, and one draw needn't show every extreme that they name: Each row of doc_ids is a permutation of 0 to 511.
All inputs are finite; a program needn't handle non-finite values.
Results may differ from a plain program's by a relative error of at most 0.0029.
Values may be sent and summed in bfloat16 or wider, within the bound.
A program may use at most 128 MiB of HBM per device.

v0:
```python
import functools
import math

import jax
import jax.numpy as jnp
from jax import lax
from jax.experimental import pallas as pl
from jax.experimental.pallas import tpu as pltpu
from jax.sharding import PartitionSpec as P

D_OUT = 64
D_IN = 64

HIGH = lax.Precision.HIGHEST
DAMPING = 0.05
MESH = pl.DeviceIdType.MESH


def gather_kernel(nz, own_ref, out, rz, rx, ry, rxh, ryh, rc, su, sd, sx, sy, sxh, syh, sc, local):
    me = lax.axis_index("doc")
    rows, cols = own_ref.shape
    half = cols // 2
    z = me // 8
    low = lax.rem(me, 8)
    core = lax.rem(low, 2)
    x = lax.rem(low // 2, 2)
    y = low // 4
    base = low - core
    col_x = base + 2 - 4 * x
    col_y = base + 4 - 8 * y
    col_xy = base + 6 - 4 * x - 8 * y
    z0 = z * 8
    to_x = z0 + col_x + core
    to_y = z0 + col_y + core
    to_c = z0 + base + 1 - core

    barrier = pltpu.get_barrier_semaphore()
    for who in (to_x, to_y, to_c):
        pl.semaphore_signal(barrier, inc=1, device_id={"doc": who}, device_id_type=MESH)

    @pl.when(z < nz - 1)
    def _():
        pl.semaphore_signal(barrier, inc=1, device_id={"doc": me + 8}, device_id_type=MESH)

    @pl.when(z > 0)
    def _():
        pl.semaphore_signal(barrier, inc=1, device_id={"doc": me - 8}, device_id_type=MESH)

    pl.semaphore_wait(barrier, 3 + jnp.minimum(z, 1) + jnp.minimum(nz - 1 - z, 1))

    def block(column, zs, c, part=None):
        row = pl.multiple_of((zs * 8 + column + c) * rows, rows)
        if part is None:
            return out.at[pl.ds(row, rows), :]
        return out.at[pl.ds(row, rows), pl.ds(part * half, half)]

    def copy(ref, dst, send, recv, who):
        return pltpu.make_async_remote_copy(
            src_ref=ref, dst_ref=dst, send_sem=send, recv_sem=recv,
            device_id={"doc": who}, device_id_type=MESH,
        )

    def up(zs, ref):
        return copy(ref, block(base, zs, core), su.at[zs], rz.at[zs], me + 8)

    def down(zs, ref):
        return copy(ref, block(base, zs, core), sd.at[zs], rz.at[zs], me - 8)

    def along_x(zs, ref):
        return copy(ref, block(base, zs, core), sx.at[zs], rx.at[zs], to_x)

    def along_y(zs, ref):
        return copy(ref, block(base, zs, core), sy.at[zs], ry.at[zs], to_y)

    def half_x(zs):
        b = block(col_y, zs, core, 1)
        return copy(b, b, sxh.at[zs], rxh.at[zs], to_x)

    def half_y(zs):
        b = block(col_x, zs, core, 0)
        return copy(b, b, syh.at[zs], ryh.at[zs], to_y)

    def other(kind, zs, ref, b):
        at = zs + kind * nz
        return copy(ref, b, sc.at[at], rc.at[at], to_c)

    own_block = block(base, z, core)
    keep = pltpu.make_async_copy(own_ref, own_block, local)

    def column_out(zs, ref):
        along_x(zs, ref).start()
        along_y(zs, ref).start()
        other(0, zs, ref, block(base, zs, core)).start()

    def steps(k, act):
        if k == 0:
            act(z, 0)
            return

        @pl.when(z - k >= 0)
        def _():
            act(z - k, 1)

        @pl.when(z + k < nz)
        def _():
            act(z + k, -1)

    def from_column(zs, way):
        b = block(base, zs, core)
        if way == 1:
            copy(b, b, su.at[zs], rz.at[zs], me - 8).wait_recv()

            @pl.when(z < nz - 1)
            def _():
                up(zs, b).start()
        else:
            copy(b, b, sd.at[zs], rz.at[zs], me + 8).wait_recv()

            @pl.when(z > 0)
            def _():
                down(zs, b).start()
        column_out(zs, b)

    def from_sides(zs, way):
        b = block(col_x, zs, core)
        copy(b, b, sx.at[zs], rx.at[zs], to_x).wait_recv()
        half_y(zs).start()
        other(1, zs, b, b).start()
        b = block(col_y, zs, core)
        copy(b, b, sy.at[zs], ry.at[zs], to_y).wait_recv()
        half_x(zs).start()
        other(2, zs, b, b).start()

    def from_corner(zs, way):
        b = block(col_xy, zs, core, 1)
        copy(b, b, sxh.at[zs], rxh.at[zs], to_x).wait_recv()
        other(3, zs, b, b).start()
        b = block(col_xy, zs, core, 0)
        copy(b, b, syh.at[zs], ryh.at[zs], to_y).wait_recv()
        other(4, zs, b, b).start()

    @pl.when(z < nz - 1)
    def _():
        up(z, own_ref).start()

    @pl.when(z > 0)
    def _():
        down(z, own_ref).start()

    column_out(z, own_ref)
    keep.start()
    for k in range(1, nz):
        steps(k, from_column)
        steps(k - 1, from_sides)
    steps(nz - 1, from_sides)
    for k in range(nz):
        steps(k, from_corner)

    keep.wait()
    for zs in range(nz):
        b = block(base, zs, core)
        along_x(zs, b).wait_send()
        along_y(zs, b).wait_send()
        half_x(zs).wait_send()
        half_y(zs).wait_send()

        @pl.when((z < nz - 1) & (zs <= z))
        def _():
            up(zs, b).wait_send()

        @pl.when((z > 0) & (zs >= z))
        def _():
            down(zs, b).wait_send()

        for kind, column, part in ((0, base, None), (1, col_x, None), (2, col_y, None), (3, col_xy, 1), (4, col_xy, 0)):
            b = block(column, zs, core, part)
            other(kind, zs, b, b).wait_send()
            b = block(column, zs, 1 - core, part)
            other(kind, zs, b, b).wait_recv()


def gather_chips(own, doc):
    nz = doc // 8
    rows, cols = own.shape
    dma = pltpu.SemaphoreType.DMA
    return pl.pallas_call(
        functools.partial(gather_kernel, nz),
        out_shape=jax.ShapeDtypeStruct((rows * doc, cols), own.dtype),
        in_specs=[pl.BlockSpec(memory_space=pl.ANY)],
        out_specs=pl.BlockSpec(memory_space=pl.ANY),
        scratch_shapes=[dma((nz,))] * 5 + [dma((5 * nz,))] + [dma((nz,))] * 6 + [dma((5 * nz,)), dma],
        compiler_params=pltpu.CompilerParams(collective_id=0, has_side_effects=True),
    )(own)


def precondition(raw, u_out, u_in, eigval):
    rotated = jnp.einsum("lac,qlab->lqcb", u_out, raw, precision=HIGH)
    rotated = jnp.einsum("lbd,lqcb->lqcd", u_in, rotated, precision=HIGH)
    scaled = rotated / (eigval[:, None] + DAMPING)
    back = jnp.einsum("lac,lqcd->lqad", u_out, scaled, precision=HIGH)
    back = jnp.einsum("lbd,lqad->qlab", u_in, back, precision=HIGH)
    return back.astype(jnp.bfloat16)


def on_device(doc, close, pool_grads, doc_ids, query_grads, u_out, u_in, eigval):
    layers, share, queries = query_grads.shape
    mine = queries // doc
    parts = query_grads.transpose(2, 0, 1).reshape(doc, mine * layers, share)
    parts = lax.all_to_all(parts, "doc", 0, 0, tiled=True)
    raw = parts.reshape(doc, mine, layers, share).transpose(1, 2, 0, 3)
    raw = raw.reshape(mine, layers, D_OUT, D_IN).astype(jnp.float32)
    own = precondition(raw, u_out, u_in, eigval).reshape(mine, layers * D_OUT * D_IN)
    if close:
        whole = gather_chips(own, doc)
    else:
        whole = lax.all_gather(own, "doc", axis=0, tiled=True)
    total = None
    width = D_OUT * D_IN
    for layer in range(layers):
        term = lax.dot_general(
            whole[:, layer * width:(layer + 1) * width], pool_grads[layer],
            (((1,), (1,)), ((), ())), preferred_element_type=jnp.float32,
        )
        total = term if total is None else total + term
    stored = lax.broadcasted_iota(jnp.int32, (pool_grads.shape[1], doc_ids.shape[1]), 0)
    pick = (stored == doc_ids[0][None, :]).astype(jnp.float32)
    total = jnp.dot(total, pick, precision=HIGH)
    total = lax.psum_scatter(total, "layer", scatter_dimension=0, tiled=True)
    return total * (1.0 / math.sqrt(D_OUT * D_IN))


def solution(mesh):
    doc = mesh.shape["doc"]
    close = mesh.shape["win"] == 1 and mesh.shape["layer"] == 1 and doc % 8 == 0
    in_specs = (
        P("layer", ("win", "doc"), None),
        P(("win", "doc"), None),
        P("layer", "doc", None),
        P("layer", None, None),
        P("layer", None, None),
        P("layer", None, None),
    )
    out_specs = P("layer", ("win", "doc"))
    return jax.shard_map(
        functools.partial(on_device, doc, close),
        mesh=mesh, in_specs=in_specs, out_specs=out_specs, check_vma=False,
    )
```

profile of v0, /device:TPU:0, one launch (start us, length us, event | category | flops | bytes accessed | tf_op | source)
XLA Modules:
  0.0 79.8 jit_solution(11479588659056827884)
XLA Ops:
  0.0 0.0 copy-start
  0.0 0.0 copy-start.2
  0.0 1.9 %copy.8 = bf16[512,2,128]{2,1,0:T(2,128)(2,1)} copy(bf16[512,2,128]{0,2,1:T(8,128)(2,1)} %bitcast.45) | data formatting | bytes 524288 | tf_op jit(solution)/shard_map/transpose | solution.py:208
  1.9 7.3 %all-to-all-start = ((bf16[32,32,128]{2,1,0:T(8,128)(2,1)}), bf16[32,32,128]{2,1,0:T(8,128)(2,1)S(1)}, u32[]{:S(2)}, u32[]{:S(2)}) async-start(bf16[32,32,128]{2,1,0:T(8,128)(2,1)} %bitcast.1), calls=%async_computation | async-start | bytes 524288 | tf_op jit(solution)/shard_map/all_to_all | solution.py:209
  9.2 0.8 %broadcast_add_fusion = f32[2,64,64]{2,1,0:T(8,128)S(1)} fusion(f32[2,64,64]{2,1,0:T(8,128)} %param.11), kind=kLoop, calls=%fused_computation.23 | loop fusion | flops 8192 | bytes 65536 | tf_op jit(solution)/shard_map/add | solution.py:199
  10.0 9.7 %all-to-all-done = bf16[32,32,128]{2,1,0:T(8,128)(2,1)S(1)} async-done(((bf16[32,32,128]{2,1,0:T(8,128)(2,1)}), bf16[32,32,128]{2,1,0:T(8,128)(2,1)S(1)}, u32[]{:S(2)}, u32[]{:S(2)}) %all-to-all-start) | async-done | bytes 262176 | tf_op jit(solution)/shard_map/all_to_all | solution.py:209
  19.8 0.1 copy.17
  19.9 0.2 reshape.16
  20.1 0.0 copy-done
  20.1 0.7 convolution_bitcast_fusion
  20.8 2.6 %convolution_divide_fusion = f32[2,16,64,64]{3,2,1,0:T(8,128)S(1)} fusion(f32[2,16,64,64]{2,3,1,0:T(8,128)S(1)} %convolution_bitcast_fusion, f32[2,64,64]{2,1,0:T(8,128)S(1)} %broadcast_add_fusion, f32[2,64,64]{2,1,0:T(8,128)} %param.10), kind=kOutput, calls=%fused_computation.10 | convolution fusion | flops 100794368 | bytes 1114112 | tf_op jit(solution)/shard_map/lbd,lqcb->lqcd/dot_general | solution.py:198
  23.5 1.1 %convolution_bitcast_fusion.1 = f32[2,16,64,64]{3,2,1,0:T(8,128)S(1)} fusion(f32[2,16,64,64]{3,2,1,0:T(8,128)S(1)} %convolution_divide_fusion, f32[2,64,64]{2,1,0:T(8,128)S(1)} %copy-done), kind=kOutput, calls=%fused_computation.9 | convolution fusion | flops 100663296 | bytes 1081344 | tf_op jit(solution)/shard_map/lac,lqcd->lqad/dot_general | solution.py:200
  24.5 0.0 copy-done.2
  24.5 1.0 %fusion.13 = bf16[16,2,64,64]{3,2,0,1:T(8,128)(2,1)S(1)} fusion(f32[2,16,64,64]{3,2,1,0:T(8,128)S(1)} %convolution_bitcast_fusion.1, f32[2,64,64]{2,1,0:T(8,128)S(1)} %copy-done.2), kind=kOutput, calls=%fused_computation.14 | convolution fusion | flops 100794368 | bytes 819200 | tf_op jit(solution)/shard_map/lbd,lqad->qlab/dot_general | solution.py:201
  25.6 1.2 %reshape.17.own_ref = bf16[16,8192]{1,0:T(8,128)(2,1)} reshape(bf16[16,2,64,64]{3,2,1,0:T(8,128)(2,1)S(1)} %copy.10) | data formatting | bytes 524288 | tf_op jit(solution)/shard_map/reshape | solution.py:212
  26.8 40.4 %shard_map.64 = bf16[512,8192]{1,0:T(8,128)(2,1)} custom-call(bf16[16,8192]{1,0:T(8,128)(2,1)} %reshape.17.own_ref), custom_call_target="tpu_custom_call" | custom-call | tf_op jit(solution)/shard_map/pallas_call | solution.py:186
  67.2 0.0 copy-start.1
  67.2 6.0 %fusion = f32[512,512]{1,0:T(8,128)S(1)} fusion(bf16[2,512,4096]{2,1,0:T(8,128)(2,1)} %param.6, bf16[512,8192]{1,0:T(8,128)(2,1)} %shard_map.64), kind=kOutput, calls=%fused_computation | convolution fusion | flops 2147483648 | bytes 9437184 | tf_op jit(solution)/shard_map/dot_general | solution.py:220
  73.2 0.0 copy-done.1
  73.2 0.0 copy-start.3
  73.2 4.5 %fusion.8 = f32[512,512]{1,0:T(8,128)S(1)} fusion(f32[512,512]{1,0:T(8,128)S(1)} %fusion, bf16[2,512,4096]{2,1,0:T(8,128)(2,1)} %param.6, bf16[512,8192]{1,0:T(8,128)(2,1)S(1)} %copy-done.1), kind=kOutput, calls=%fused_computation.12 | convolution fusion | flops 2147745792 | bytes 10485760 | tf_op jit(solution)/shard_map/dot_general | solution.py:220
  77.8 0.0 copy-done.3
  77.8 2.0 %convolution_multiply_fusion = f32[512,512]{1,0:T(8,128)} fusion(f32[512,512]{1,0:T(8,128)S(1)} %fusion.8, s32[512]{0:T(512)S(1)} %bitcast.46), kind=kOutput, calls=%fused_computation.11 | convolution fusion | flops 1611137024 | bytes 2099200 | tf_op jit(solution)/shard_map/dot_general | solution.py:227
  (1 shorter events, 0.0 us)
Async XLA Ops:
  0.0 20.1 %copy-start = (f32[2,64,64]{2,1,0:T(8,128)S(1)}, f32[2,64,64]{2,1,0:T(8,128)}, u32[]{:S(2)}) copy-start(f32[2,64,64]{2,1,0:T(8,128)} %param.9) | copy-start | bytes 98308
  0.0 24.5 %copy-start.2 = (f32[2,64,64]{2,1,0:T(8,128)S(1)}, f32[2,64,64]{2,1,0:T(8,128)}, u32[]{:S(2)}) copy-start(f32[2,64,64]{2,1,0:T(8,128)} %param.10) | copy-start | bytes 98308
  1.9 17.9 %all-to-all-start = ((bf16[32,32,128]{2,1,0:T(8,128)(2,1)}), bf16[32,32,128]{2,1,0:T(8,128)(2,1)S(1)}, u32[]{:S(2)}, u32[]{:S(2)}) async-start(bf16[32,32,128]{2,1,0:T(8,128)(2,1)} %bitcast.1), calls=%async_computation | async-start | bytes 524288 | tf_op jit(solution)/shard_map/all_to_all | solution.py:209
  67.2 6.0 %copy-start.1 = (bf16[512,8192]{1,0:T(8,128)(2,1)S(1)}, bf16[512,8192]{1,0:T(8,128)(2,1)}, u32[]{:S(2)}) copy-start(bf16[512,8192]{1,0:T(8,128)(2,1)} %shard_map.64) | copy-start | bytes 25165828
  73.2 4.6 %copy-start.3 = (s32[1,512]{1,0:T(1,128)S(1)}, s32[1,512]{1,0:T(1,128)}, u32[]{:S(2)}) copy-start(s32[1,512]{1,0:T(1,128)} %param.7) | copy-start | bytes 6148
where the time goes:
time: 80.1 us; the launch traced here: 79.8 us
  Pallas kernels  40.4 us (50%)
  matrix products  17.9 us (22%)
  waiting for transfers between devices  9.75 us (12%)
  starting transfers between devices  7.3 us (9%)
  local copies, waits for them, and re-layouts  3.43 us (4%)
  other arithmetic  0.85 us (1%)
    pallas_call x1, Pallas kernels, gather_chips(): pl.pallas_call(functools.partial(gather_kernel, nz), out_shape=jax.ShapeD...  40.4 us
    dot_general x2, matrix products, on_device(): lax.dot_general(whole[:, layer * width:(layer + 1) * width], pool_grads[l...  10.5 us
    all_to_all x1, waiting for transfers between devices, on_device(): parts = lax.all_to_all(parts, 'doc', 0, 0, tiled=True)  9.75 us
    all_to_all x1, starting transfers between devices, on_device(): parts = lax.all_to_all(parts, 'doc', 0, 0, tiled=True)  7.3 us
    dot_general x1, matrix products, precondition(): rotated = jnp.einsum('lbd,lqcb->lqcd', u_in, rotated, precision=HIGH)  2.64 us
    dot_general x1, matrix products, on_device(): total = jnp.dot(total, pick, precision=HIGH)  2.03 us
    transpose x1, local copies, waits for them, and re-layouts, on_device(): parts = query_grads.transpose(2, 0, 1).reshape(doc, mine * layers, share)  1.86 us
  transfers between devices with their start and end apart: 1, of which 1 were waited for; matrix products, arithmetic and copies ran while one was open for 1% of the time, Pallas kernels for 0%

commit v1 on v0

--- a/solution.py
+++ b/solution.py
@@ -193,6 +193,93 @@
     )(own)
 
 
+def exchange_kernel(doc, parts, out, send, recv, local):
+    me = lax.axis_index("doc")
+    barrier = pltpu.get_barrier_semaphore()
+
+    @pl.loop(1, doc)
+    def _(j):
+        pl.semaphore_signal(barrier, inc=1, device_id={"doc": lax.rem(me + j, doc)}, device_id_type=MESH)
+
+    pl.semaphore_wait(barrier, doc - 1)
+    keep = pltpu.make_async_copy(parts.at[me], out.at[me], local)
+    keep.start()
+
+    def copy(j, to, at):
+        return pltpu.make_async_remote_copy(
+            src_ref=parts.at[to], dst_ref=out.at[at], send_sem=send.at[j], recv_sem=recv.at[j],
+            device_id={"doc": to}, device_id_type=MESH,
+        )
+
+    @pl.loop(1, doc)
+    def _(j):
+        copy(j, lax.rem(me + j, doc), me).start()
+
+    keep.wait()
+
+    @pl.loop(1, doc)
+    def _(j):
+        copy(j, lax.rem(me + j, doc), lax.rem(me - j + doc, doc)).wait()
+
+
+def exchange(parts, doc):
+    dma = pltpu.SemaphoreType.DMA
+    return pl.pallas_call(
+        functools.partial(exchange_kernel, doc),
+        out_shape=jax.ShapeDtypeStruct(parts.shape, parts.dtype),
+        in_specs=[pl.BlockSpec(memory_space=pl.ANY)],
+        out_specs=pl.BlockSpec(memory_space=pl.ANY),
+        scratch_shapes=[dma((doc,)), dma((doc,)), dma],
+        compiler_params=pltpu.CompilerParams(collective_id=1, has_side_effects=True),
+    )(parts)
+
+
+def score_kernel(ids, prepared, docs, out):
+    at = pl.program_id(0)
+
+    @pl.when(at == 0)
+    def _():
+        out[...] = jnp.zeros_like(out)
+
+    out[...] += lax.dot_general(
+        prepared[...], docs[0], (((1,), (1,)), ((), ())), preferred_element_type=jnp.float32
+    )
+
+    @pl.when(at == pl.num_programs(0) - 1)
+    def _():
+        stored = lax.broadcasted_iota(jnp.int32, (docs.shape[1], ids.shape[1]), 0)
+        pick = jnp.where(stored == ids[...], 1.0, 0.0).astype(jnp.bfloat16)
+        rest = out[...]
+        total = None
+        for _ in range(3):
+            part = rest.astype(jnp.bfloat16)
+            rest = rest - part.astype(jnp.float32)
+            term = jnp.dot(part, pick, preferred_element_type=jnp.float32)
+            total = term if total is None else total + term
+        out[...] = total * (1.0 / math.sqrt(D_OUT * D_IN))
+
+
+def score(ids, prepared, docs):
+    layers, stored, width = docs.shape
+    queries = prepared.shape[0]
+    depth = 1024
+    cuts = width // depth
+    return pl.pallas_call(
+        score_kernel,
+        grid=(layers * cuts,),
+        out_shape=jax.ShapeDtypeStruct((queries, ids.shape[1]), jnp.float32),
+        in_specs=[
+            pl.BlockSpec(ids.shape, lambda k: (0, 0)),
+            pl.BlockSpec((queries, depth), lambda k: (0, k)),
+            pl.BlockSpec((1, stored, depth), lambda k: (k // cuts, 0, k % cuts)),
+        ],
+        out_specs=pl.BlockSpec((queries, ids.shape[1]), lambda k: (0, 0)),
+        compiler_params=pltpu.CompilerParams(
+            dimension_semantics=("arbitrary",), vmem_limit_bytes=32 * 1024 * 1024
+        ),
+    )(ids, prepared, docs)
+
+
 def precondition(raw, u_out, u_in, eigval):
     rotated = jnp.einsum("lac,qlab->lqcb", u_out, raw, precision=HIGH)
     rotated = jnp.einsum("lbd,lqcb->lqcd", u_in, rotated, precision=HIGH)
@@ -206,7 +293,10 @@
     layers, share, queries = query_grads.shape
     mine = queries // doc
     parts = query_grads.transpose(2, 0, 1).reshape(doc, mine * layers, share)
-    parts = lax.all_to_all(parts, "doc", 0, 0, tiled=True)
+    if close:
+        parts = exchange(parts, doc)
+    else:
+        parts = lax.all_to_all(parts, "doc", 0, 0, tiled=True)
     raw = parts.reshape(doc, mine, layers, share).transpose(1, 2, 0, 3)
     raw = raw.reshape(mine, layers, D_OUT, D_IN).astype(jnp.float32)
     own = precondition(raw, u_out, u_in, eigval).reshape(mine, layers * D_OUT * D_IN)
@@ -214,19 +304,8 @@
         whole = gather_chips(own, doc)
     else:
         whole = lax.all_gather(own, "doc", axis=0, tiled=True)
-    total = None
-    width = D_OUT * D_IN
-    for layer in range(layers):
-        term = lax.dot_general(
-            whole[:, layer * width:(layer + 1) * width], pool_grads[layer],
-            (((1,), (1,)), ((), ())), preferred_element_type=jnp.float32,
-        )
-        total = term if total is None else total + term
-    stored = lax.broadcasted_iota(jnp.int32, (pool_grads.shape[1], doc_ids.shape[1]), 0)
-    pick = (stored == doc_ids[0][None, :]).astype(jnp.float32)
-    total = jnp.dot(total, pick, precision=HIGH)
-    total = lax.psum_scatter(total, "layer", scatter_dimension=0, tiled=True)
-    return total * (1.0 / math.sqrt(D_OUT * D_IN))
+    total = score(doc_ids, whole, pool_grads)
+    return lax.psum_scatter(total, "layer", scatter_dimension=0, tiled=True)
 
 
 def solution(mesh):

time: 80.1 us -> 83.1 us (1.037)
  Pallas kernels: 40.4 us -> 65.2 us
  matrix products: 17.9 us -> 5.41 us
  waiting for transfers between devices: 9.75 us -> 0 us
  local copies, waits for them, and re-layouts: 3.43 us -> 11.1 us
  starting transfers between devices: 7.3 us -> 0 us
    pallas_call x0 -> x2, Pallas kernels: none -> 21.9 us  [the longest x1 12.6 us: exchange(): pl.pallas_call(functools.partial(exchange_kernel, doc), out_shape=jax.Sha...]
    dot_general x3 -> x0, matrix products: 12.5 us -> none  [the longest x2 10.5 us: on_device(): lax.dot_general(whole[:, layer * width:(layer + 1) * width], pool_grads[l...]
    all_to_all x1 -> x0, waiting for transfers between devices: 9.75 us -> none  [on_device(): parts = lax.all_to_all(parts, 'doc', 0, 0, tiled=True)]
    all_to_all x1 -> x0, starting transfers between devices: 7.3 us -> none  [on_device(): parts = lax.all_to_all(parts, 'doc', 0, 0, tiled=True)]
    unnamed x8 -> x10, local copies, waits for them, and re-layouts: 0.02 us -> 6.77 us
    pallas_call x1, Pallas kernels: 40.4 us -> 43.3 us  [gather_chips(): pl.pallas_call(functools.partial(gather_kernel, nz), out_shape=jax.ShapeD...]
    reshape x1, local copies, waits for them, and re-layouts: 0.1 us -> 1.05 us  [on_device(): raw = parts.reshape(doc, mine, layers, share).transpose(1, 2, 0, 3)]
  transfers between devices with their start and end apart: 1 -> 0, of which waited for: 1 -> 0; matrix products, arithmetic and copies ran while one was open for 1% -> 0% of each run, Pallas kernels for 0% -> 0%
where the time goes in v1:
time: 83.1 us; the launch traced here: 82.8 us
  Pallas kernels  65.2 us (78%)
  local copies, waits for them, and re-layouts  11.1 us (13%)
  matrix products  5.41 us (7%)
  other arithmetic  0.88 us (1%)
    pallas_call x1, Pallas kernels, gather_chips(): pl.pallas_call(functools.partial(gather_kernel, nz), out_shape=jax.ShapeD...  43.3 us
    pallas_call x1, Pallas kernels, exchange(): pl.pallas_call(functools.partial(exchange_kernel, doc), out_shape=jax.Sha...  12.6 us
    pallas_call x1, Pallas kernels, score(): pl.pallas_call(score_kernel, grid=(layers * cuts,), out_shape=jax.ShapeDt...  9.35 us
    unnamed x10, local copies, waits for them, and re-layouts  6.77 us
    dot_general x1, matrix products, precondition(): rotated = jnp.einsum('lbd,lqcb->lqcd', u_in, rotated, precision=HIGH)  2.64 us
    transpose x1, local copies, waits for them, and re-layouts, on_device(): parts = query_grads.transpose(2, 0, 1).reshape(doc, mine * layers, share)  1.82 us

profile of v1, /device:TPU:0, one launch (start us, length us, event | category | flops | bytes accessed | tf_op | source)
XLA Modules:
  0.0 82.8 jit_solution(2641725732725452811)
XLA Ops:
  0.0 0.0 copy-start
  0.0 0.0 copy-start.4
  0.0 0.9 %broadcast_add_fusion = f32[2,64,64]{2,1,0:T(8,128)S(1)} fusion(f32[2,64,64]{2,1,0:T(8,128)} %param.11), kind=kLoop, calls=%fused_computation.11 | loop fusion | flops 8192 | bytes 65536 | tf_op jit(solution)/shard_map/add | solution.py:286
  0.9 1.8 %copy.9 = bf16[512,2,128]{2,1,0:T(2,128)(2,1)} copy(bf16[512,2,128]{0,2,1:T(8,128)(2,1)} %bitcast.36) | data formatting | bytes 524288 | tf_op jit(solution)/shard_map/transpose | solution.py:295
  2.7 12.6 %shard_map.64 = bf16[32,32,128]{2,1,0:T(8,128)(2,1)} custom-call(bf16[32,32,128]{2,1,0:T(8,128)(2,1)} %bitcast.35), custom_call_target="tpu_custom_call" | custom-call | tf_op jit(solution)/shard_map/pallas_call | solution.py:227
  15.3 1.1 %copy.18 = bf16[32,16,2,128]{3,0,2,1:T(8,128)(2,1)S(1)} copy(bf16[32,16,2,128]{3,2,1,0:T(2,128)(2,1)} %bitcast.34) | data formatting | bytes 524288 | tf_op jit(solution)/shard_map/reshape | solution.py:300
  16.4 0.2 reshape.16
  16.6 0.0 copy-done
  16.6 0.7 convolution_bitcast_fusion
  17.3 0.0 copy-start.3
  17.3 2.6 %convolution_divide_fusion = f32[2,16,64,64]{3,2,1,0:T(8,128)S(1)} fusion(f32[2,16,64,64]{2,3,1,0:T(8,128)S(1)} %convolution_bitcast_fusion, f32[2,64,64]{2,1,0:T(8,128)S(1)} %broadcast_add_fusion, f32[2,64,64]{2,1,0:T(8,128)} %param.10), kind=kOutput, calls=%fused_computation.2 | convolution fusion | flops 100794368 | bytes 1114112 | tf_op jit(solution)/shard_map/lbd,lqcb->lqcd/dot_general | solution.py:285
  20.0 1.1 %convolution_bitcast_fusion.1 = f32[2,16,64,64]{3,2,1,0:T(8,128)S(1)} fusion(f32[2,16,64,64]{3,2,1,0:T(8,128)S(1)} %convolution_divide_fusion, f32[2,64,64]{2,1,0:T(8,128)S(1)} %copy-done), kind=kOutput, calls=%fused_computation.1 | convolution fusion | flops 100663296 | bytes 1081344 | tf_op jit(solution)/shard_map/lac,lqcd->lqad/dot_general | solution.py:287
  21.0 0.0 copy-done.4
  21.0 1.0 %fusion = bf16[16,2,64,64]{3,2,0,1:T(8,128)(2,1)S(1)} fusion(f32[2,16,64,64]{3,2,1,0:T(8,128)S(1)} %convolution_bitcast_fusion.1, f32[2,64,64]{2,1,0:T(8,128)S(1)} %copy-done.4), kind=kOutput, calls=%fused_computation.4 | convolution fusion | flops 100794368 | bytes 819200 | tf_op jit(solution)/shard_map/lbd,lqad->qlab/dot_general | solution.py:288
  22.1 1.2 %reshape.17.own_ref = bf16[16,8192]{1,0:T(8,128)(2,1)} reshape(bf16[16,2,64,64]{3,2,1,0:T(8,128)(2,1)S(1)} %copy.11) | data formatting | bytes 524288 | tf_op jit(solution)/shard_map/reshape | solution.py:302
  23.3 43.3 %shard_map.65.prepared = bf16[512,8192]{1,0:T(8,128)(2,1)} custom-call(bf16[16,8192]{1,0:T(8,128)(2,1)} %reshape.17.own_ref), custom_call_target="tpu_custom_call" | custom-call | tf_op jit(solution)/shard_map/pallas_call | solution.py:186
  66.6 0.0 copy-done.3
  66.6 0.0 copy-start.1
  66.7 3.4 %copy-done.1 = bf16[512,8192]{1,0:T(8,128)(2,1)S(1)} copy-done((bf16[512,8192]{1,0:T(8,128)(2,1)S(1)}, bf16[512,8192]{1,0:T(8,128)(2,1)}, u32[]{:S(2)}) %copy-start.1) | copy-done | bytes 8388632
  70.0 0.0 copy-start.2
  70.0 3.4 %copy-done.2 = bf16[2,512,4096]{2,1,0:T(8,128)(2,1)S(1)} copy-done((bf16[2,512,4096]{2,1,0:T(8,128)(2,1)S(1)}, bf16[2,512,4096]{2,1,0:T(8,128)(2,1)}, u32[]{:S(2)}) %copy-start.2) | copy-done | bytes 8388632
  73.4 9.3 %shard_map.66 = f32[512,512]{1,0:T(8,128)} custom-call(s32[1,512]{1,0:T(1,128)S(1)} %copy-done.3, bf16[512,8192]{1,0:T(8,128)(2,1)S(1)} %copy-done.1, bf16[2,512,4096]{2,1,0:T(8,128)(2,1)S(1)} %copy-done.2), custom_call_target="tpu_custom_call" | custom-call | tf_op jit(solution)/shard_map/pallas_call | solution.py:267
  (1 shorter events, 0.0 us)
Async XLA Ops:
  0.0 16.6 %copy-start = (f32[2,64,64]{2,1,0:T(8,128)S(1)}, f32[2,64,64]{2,1,0:T(8,128)}, u32[]{:S(2)}) copy-start(f32[2,64,64]{2,1,0:T(8,128)} %param.9) | copy-start | bytes 98308
  0.0 21.0 %copy-start.4 = (f32[2,64,64]{2,1,0:T(8,128)S(1)}, f32[2,64,64]{2,1,0:T(8,128)}, u32[]{:S(2)}) copy-start(f32[2,64,64]{2,1,0:T(8,128)} %param.10) | copy-start | bytes 98308
  17.3 49.4 %copy-start.3 = (s32[1,512]{1,0:T(1,128)S(1)}, s32[1,512]{1,0:T(1,128)}, u32[]{:S(2)}) copy-start(s32[1,512]{1,0:T(1,128)} %ids.1) | copy-start | bytes 6148
  66.6 3.4 %copy-start.1 = (bf16[512,8192]{1,0:T(8,128)(2,1)S(1)}, bf16[512,8192]{1,0:T(8,128)(2,1)}, u32[]{:S(2)}) copy-start(bf16[512,8192]{1,0:T(8,128)(2,1)} %shard_map.65.prepared) | copy-start | bytes 25165828
  70.0 3.4 %copy-start.2 = (bf16[2,512,4096]{2,1,0:T(8,128)(2,1)S(1)}, bf16[2,512,4096]{2,1,0:T(8,128)(2,1)}, u32[]{:S(2)}) copy-start(bf16[2,512,4096]{2,1,0:T(8,128)(2,1)} %docs.1) | copy-start | bytes 25165828

commit v2 on v1

--- a/solution.py
+++ b/solution.py
@@ -262,7 +262,7 @@
 def score(ids, prepared, docs):
     layers, stored, width = docs.shape
     queries = prepared.shape[0]
-    depth = 1024
+    depth = 2048
     cuts = width // depth
     return pl.pallas_call(
         score_kernel,
@@ -275,7 +275,7 @@
         ],
         out_specs=pl.BlockSpec((queries, ids.shape[1]), lambda k: (0, 0)),
         compiler_params=pltpu.CompilerParams(
-            dimension_semantics=("arbitrary",), vmem_limit_bytes=32 * 1024 * 1024
+            dimension_semantics=("arbitrary",), vmem_limit_bytes=60 * 1024 * 1024
         ),
     )(ids, prepared, docs)
 

time: 83.1 us -> 77.5 us (0.933)
  local copies, waits for them, and re-layouts: 11.1 us -> 4.34 us
  Pallas kernels: 65.2 us -> 66.5 us
    unnamed x10 -> x4, local copies, waits for them, and re-layouts: 6.77 us -> 0.01 us
    pallas_call x1, Pallas kernels: 9.35 us -> 10.6 us  [score(): pl.pallas_call(score_kernel, grid=(layers * cuts,), out_shape=jax.ShapeDt...]
where the time goes in v2:
time: 77.5 us; the launch traced here: 77.2 us
  Pallas kernels  66.5 us (86%)
  matrix products  5.41 us (7%)
  local copies, waits for them, and re-layouts  4.34 us (6%)
  other arithmetic  0.88 us (1%)
    pallas_call x1, Pallas kernels, gather_chips(): pl.pallas_call(functools.partial(gather_kernel, nz), out_shape=jax.ShapeD...  43.3 us
    pallas_call x1, Pallas kernels, exchange(): pl.pallas_call(functools.partial(exchange_kernel, doc), out_shape=jax.Sha...  12.6 us
    pallas_call x1, Pallas kernels, score(): pl.pallas_call(score_kernel, grid=(layers * cuts,), out_shape=jax.ShapeDt...  10.6 us
    dot_general x1, matrix products, precondition(): rotated = jnp.einsum('lbd,lqcb->lqcd', u_in, rotated, precision=HIGH)  2.64 us
    transpose x1, local copies, waits for them, and re-layouts, on_device(): parts = query_grads.transpose(2, 0, 1).reshape(doc, mine * layers, share)  1.82 us

profile of v2, /device:TPU:0, one launch (start us, length us, event | category | flops | bytes accessed | tf_op | source)
XLA Modules:
  0.0 77.2 jit_solution(2066946087605399294)
XLA Ops:
  0.0 0.0 copy-start
  0.0 0.0 copy-start.1
  0.0 0.9 %broadcast_add_fusion = f32[2,64,64]{2,1,0:T(8,128)S(1)} fusion(f32[2,64,64]{2,1,0:T(8,128)} %param.11), kind=kLoop, calls=%fused_computation.11 | loop fusion | flops 8192 | bytes 65536 | tf_op jit(solution)/shard_map/add | solution.py:286
  0.9 1.8 %copy.9 = bf16[512,2,128]{2,1,0:T(2,128)(2,1)} copy(bf16[512,2,128]{0,2,1:T(8,128)(2,1)} %bitcast.36) | data formatting | bytes 524288 | tf_op jit(solution)/shard_map/transpose | solution.py:295
  2.7 12.6 %shard_map.64 = bf16[32,32,128]{2,1,0:T(8,128)(2,1)} custom-call(bf16[32,32,128]{2,1,0:T(8,128)(2,1)} %bitcast.35), custom_call_target="tpu_custom_call" | custom-call | tf_op jit(solution)/shard_map/pallas_call | solution.py:227
  15.3 1.1 %copy.18 = bf16[32,16,2,128]{3,0,2,1:T(8,128)(2,1)S(1)} copy(bf16[32,16,2,128]{3,2,1,0:T(2,128)(2,1)} %bitcast.34) | data formatting | bytes 524288 | tf_op jit(solution)/shard_map/reshape | solution.py:300
  16.4 0.2 reshape.16
  16.6 0.0 copy-done
  16.6 0.7 convolution_bitcast_fusion
  17.3 2.6 %convolution_divide_fusion = f32[2,16,64,64]{3,2,1,0:T(8,128)S(1)} fusion(f32[2,16,64,64]{2,3,1,0:T(8,128)S(1)} %convolution_bitcast_fusion, f32[2,64,64]{2,1,0:T(8,128)S(1)} %broadcast_add_fusion, f32[2,64,64]{2,1,0:T(8,128)} %param.10), kind=kOutput, calls=%fused_computation.2 | convolution fusion | flops 100794368 | bytes 1114112 | tf_op jit(solution)/shard_map/lbd,lqcb->lqcd/dot_general | solution.py:285
  19.9 1.1 %convolution_bitcast_fusion.1 = f32[2,16,64,64]{3,2,1,0:T(8,128)S(1)} fusion(f32[2,16,64,64]{3,2,1,0:T(8,128)S(1)} %convolution_divide_fusion, f32[2,64,64]{2,1,0:T(8,128)S(1)} %copy-done), kind=kOutput, calls=%fused_computation.1 | convolution fusion | flops 100663296 | bytes 1081344 | tf_op jit(solution)/shard_map/lac,lqcd->lqad/dot_general | solution.py:287
  21.0 0.0 copy-done.1
  21.0 1.0 %fusion = bf16[16,2,64,64]{3,2,0,1:T(8,128)(2,1)S(1)} fusion(f32[2,16,64,64]{3,2,1,0:T(8,128)S(1)} %convolution_bitcast_fusion.1, f32[2,64,64]{2,1,0:T(8,128)S(1)} %copy-done.1), kind=kOutput, calls=%fused_computation.4 | convolution fusion | flops 100794368 | bytes 819200 | tf_op jit(solution)/shard_map/lbd,lqad->qlab/dot_general | solution.py:288
  22.1 1.2 %reshape.17.own_ref = bf16[16,8192]{1,0:T(8,128)(2,1)} reshape(bf16[16,2,64,64]{3,2,1,0:T(8,128)(2,1)S(1)} %copy.11) | data formatting | bytes 524288 | tf_op jit(solution)/shard_map/reshape | solution.py:302
  23.3 43.3 %shard_map.65.prepared = bf16[512,8192]{1,0:T(8,128)(2,1)} custom-call(bf16[16,8192]{1,0:T(8,128)(2,1)} %reshape.17.own_ref), custom_call_target="tpu_custom_call" | custom-call | tf_op jit(solution)/shard_map/pallas_call | solution.py:186
  66.6 10.6 %shard_map.66 = f32[512,512]{1,0:T(8,128)} custom-call(s32[1,512]{1,0:T(1,128)} %ids.1, bf16[512,8192]{1,0:T(8,128)(2,1)} %shard_map.65.prepared, bf16[2,512,4096]{2,1,0:T(8,128)(2,1)} %docs.1), custom_call_target="tpu_custom_call" | custom-call | tf_op jit(solution)/shard_map/pallas_call | solution.py:267
  (1 shorter events, 0.0 us)
Async XLA Ops:
  0.0 16.6 %copy-start = (f32[2,64,64]{2,1,0:T(8,128)S(1)}, f32[2,64,64]{2,1,0:T(8,128)}, u32[]{:S(2)}) copy-start(f32[2,64,64]{2,1,0:T(8,128)} %param.9) | copy-start | bytes 98308
  0.0 21.0 %copy-start.1 = (f32[2,64,64]{2,1,0:T(8,128)S(1)}, f32[2,64,64]{2,1,0:T(8,128)}, u32[]{:S(2)}) copy-start(f32[2,64,64]{2,1,0:T(8,128)} %param.10) | copy-start | bytes 98308

commit v3 on v2

--- a/solution.py
+++ b/solution.py
@@ -11,7 +11,7 @@
 D_OUT = 64
 D_IN = 64
 
-HIGH = lax.Precision.HIGHEST
+HIGH = lax.Precision.HIGH
 DAMPING = 0.05
 MESH = pl.DeviceIdType.MESH
 
@@ -262,7 +262,7 @@
 def score(ids, prepared, docs):
     layers, stored, width = docs.shape
     queries = prepared.shape[0]
-    depth = 2048
+    depth = 1024
     cuts = width // depth
     return pl.pallas_call(
         score_kernel,
@@ -283,7 +283,7 @@
 def precondition(raw, u_out, u_in, eigval):
     rotated = jnp.einsum("lac,qlab->lqcb", u_out, raw, precision=HIGH)
     rotated = jnp.einsum("lbd,lqcb->lqcd", u_in, rotated, precision=HIGH)
-    scaled = rotated / (eigval[:, None] + DAMPING)
+    scaled = rotated * (1.0 / (eigval + DAMPING))[:, None]
     back = jnp.einsum("lac,lqcd->lqad", u_out, scaled, precision=HIGH)
     back = jnp.einsum("lbd,lqad->qlab", u_in, back, precision=HIGH)
     return back.astype(jnp.bfloat16)

time: 77.5 us -> 77.6 us (level)
  matrix products: 5.41 us -> 3.49 us
  Pallas kernels: 66.5 us -> 68.4 us
    pallas_call x1, Pallas kernels: 10.6 us -> 12.5 us  [score(): pl.pallas_call(score_kernel, grid=(layers * cuts,), out_shape=jax.ShapeDt...]
    div x0 -> x1, other arithmetic: none -> 0.89 us  [precondition(): scaled = rotated * (1.0 / (eigval + DAMPING))[:, None]]
    add x1 -> x0, other arithmetic: 0.88 us -> none  [precondition(): scaled = rotated / (eigval[:, None] + DAMPING)]
    dot_general x1, matrix products: 2.64 us -> 1.83 us  [precondition(): rotated = jnp.einsum('lbd,lqcb->lqcd', u_in, rotated, precision=HIGH)]
where the time goes in v3:
time: 77.6 us; the launch traced here: 77.2 us
  Pallas kernels  68.4 us (88%)
  local copies, waits for them, and re-layouts  4.34 us (6%)
  matrix products  3.49 us (4%)
  other arithmetic  0.89 us (1%)
    pallas_call x1, Pallas kernels, gather_chips(): pl.pallas_call(functools.partial(gather_kernel, nz), out_shape=jax.ShapeD...  43.3 us
    pallas_call x1, Pallas kernels, exchange(): pl.pallas_call(functools.partial(exchange_kernel, doc), out_shape=jax.Sha...  12.6 us
    pallas_call x1, Pallas kernels, score(): pl.pallas_call(score_kernel, grid=(layers * cuts,), out_shape=jax.ShapeDt...  12.5 us
    dot_general x1, matrix products, precondition(): rotated = jnp.einsum('lbd,lqcb->lqcd', u_in, rotated, precision=HIGH)  1.83 us
    transpose x1, local copies, waits for them, and re-layouts, on_device(): parts = query_grads.transpose(2, 0, 1).reshape(doc, mine * layers, share)  1.82 us

profile of v3, /device:TPU:0, one launch (start us, length us, event | category | flops | bytes accessed | tf_op | source)
XLA Modules:
  0.0 77.2 jit_solution(7903531310525928467)
XLA Ops:
  0.0 0.0 copy-start
  0.0 0.0 copy-start.1
  0.0 0.9 %add_divide_fusion = f32[2,64,64]{2,1,0:T(8,128)S(1)} fusion(f32[2,64,64]{2,1,0:T(8,128)} %param.11), kind=kLoop, calls=%fused_computation.11 | loop fusion | flops 16384 | bytes 65536 | tf_op jit(solution)/shard_map/div | solution.py:286
  0.9 1.8 %copy.9 = bf16[512,2,128]{2,1,0:T(2,128)(2,1)} copy(bf16[512,2,128]{0,2,1:T(8,128)(2,1)} %bitcast.36) | data formatting | bytes 524288 | tf_op jit(solution)/shard_map/transpose | solution.py:295
  2.7 12.6 %shard_map.64 = bf16[32,32,128]{2,1,0:T(8,128)(2,1)} custom-call(bf16[32,32,128]{2,1,0:T(8,128)(2,1)} %bitcast.35), custom_call_target="tpu_custom_call" | custom-call | tf_op jit(solution)/shard_map/pallas_call | solution.py:227
  15.3 1.1 %copy.18 = bf16[32,16,2,128]{3,0,2,1:T(8,128)(2,1)S(1)} copy(bf16[32,16,2,128]{3,2,1,0:T(2,128)(2,1)} %bitcast.34) | data formatting | bytes 524288 | tf_op jit(solution)/shard_map/reshape | solution.py:300
  16.4 0.2 reshape.15
  16.6 0.0 copy-done
  16.6 0.5 convolution_bitcast_fusion
  17.2 1.8 %convolution_multiply_fusion = f32[2,16,64,64]{3,2,1,0:T(8,128)S(1)} fusion(f32[2,16,64,64]{2,3,1,0:T(8,128)S(1)} %convolution_bitcast_fusion, f32[2,64,64]{2,1,0:T(8,128)S(1)} %add_divide_fusion, f32[2,64,64]{2,1,0:T(8,128)} %param.10), kind=kOutput, calls=%fused_computation.2 | convolution fusion | flops 50462720 | bytes 1114112 | tf_op jit(solution)/shard_map/lbd,lqcb->lqcd/dot_general | solution.py:285
  19.0 0.6 convolution_bitcast_fusion.1
  19.6 0.0 copy-done.1
  19.6 0.6 fusion
  20.2 1.2 %reshape.16.own_ref = bf16[16,8192]{1,0:T(8,128)(2,1)} reshape(bf16[16,2,64,64]{3,2,1,0:T(8,128)(2,1)S(1)} %copy.11) | data formatting | bytes 524288 | tf_op jit(solution)/shard_map/reshape | solution.py:302
  21.4 43.3 %shard_map.65.prepared = bf16[512,8192]{1,0:T(8,128)(2,1)} custom-call(bf16[16,8192]{1,0:T(8,128)(2,1)} %reshape.16.own_ref), custom_call_target="tpu_custom_call" | custom-call | tf_op jit(solution)/shard_map/pallas_call | solution.py:186
  64.7 12.5 %shard_map.66 = f32[512,512]{1,0:T(8,128)} custom-call(s32[1,512]{1,0:T(1,128)} %ids.1, bf16[512,8192]{1,0:T(8,128)(2,1)} %shard_map.65.prepared, bf16[2,512,4096]{2,1,0:T(8,128)(2,1)} %docs.1), custom_call_target="tpu_custom_call" | custom-call | tf_op jit(solution)/shard_map/pallas_call | solution.py:267
  (1 shorter events, 0.0 us)
Async XLA Ops:
  0.0 16.6 %copy-start = (f32[2,64,64]{2,1,0:T(8,128)S(1)}, f32[2,64,64]{2,1,0:T(8,128)}, u32[]{:S(2)}) copy-start(f32[2,64,64]{2,1,0:T(8,128)} %param.9) | copy-start | bytes 98308
  0.0 19.6 %copy-start.1 = (f32[2,64,64]{2,1,0:T(8,128)S(1)}, f32[2,64,64]{2,1,0:T(8,128)}, u32[]{:S(2)}) copy-start(f32[2,64,64]{2,1,0:T(8,128)} %param.10) | copy-start | bytes 98308
